TPU v7x, 32 devices: a whole 2x2x4 slice. The times are simulated.
32 devices in a mesh: fsdp: 16 (over z, y, x), tp: 2 (over core).
Axes of the slice: x: 2, y: 2, z: 4, core: 2. Of those that a mesh axis runs over, the one named last changes fastest.
Arguments:
- tokens: bfloat16 [12608, 768], P(('fsdp', 'tp')), may hold values from -6 to 6
- cotangent: bfloat16 [12608, 768], P(('fsdp', 'tp')), may hold values from -6 to 6
- image_counts: int32 [16], P('fsdp'), may hold values from 1 to 4, as said below
- w_qkv: bfloat16 [3, 768, 768], P(None, 'fsdp', 'tp'), may hold values from -0.21875 to 0.21875
- b_query: float32 [768], P('tp'), may hold values from -3 to 3
- b_value: float32 [768], P('tp'), may hold values from -3 to 3
- w_out: bfloat16 [768, 768], P('tp', 'fsdp'), may hold values from -0.75 to 0.75
- b_out: float32 [768], replicated, may hold values from -3 to 3
- w_up: bfloat16 [768, 3072], P('fsdp', 'tp'), may hold values from -0.21875 to 0.21875
- b_up: float32 [3072], P('tp'), may hold values from -3 to 3
- w_down: bfloat16 [3072, 768], P('tp', 'fsdp'), may hold values from -0.15625 to 0.15625
- b_down: float32 [768], replicated, may hold values from -3 to 3
- gain_one: float32 [768], replicated, may hold values from 0.1 to 1.9
- shift_one: float32 [768], replicated, may hold values from -3 to 3
- gain_two: float32 [768], replicated, may hold values from 0.1 to 1.9
- shift_two: float32 [768], replicated, may hold values from -3 to 3
Outputs:
- block_out: bfloat16 [12608, 768], P(('fsdp', 'tp'))
- grad_tokens: float32 [12608, 768], P(('fsdp', 'tp'))
- grad_qkv: float32 [3, 768, 768], P(None, 'fsdp', 'tp')
- grad_out: float32 [768, 768], P('tp', 'fsdp')
- grad_up: float32 [768, 3072], P('fsdp', 'tp')
- grad_down: float32 [3072, 768], P('tp', 'fsdp')
- grad_b_query: float32 [768], P('tp')
- grad_b_value: float32 [768], P('tp')
- grad_b_out: float32 [768], replicated
- grad_b_up: float32 [3072], P('tp')
- grad_b_down: float32 [768], replicated
- grad_gain_one: float32 [768], replicated
- grad_shift_one: float32 [768], replicated
- grad_gain_two: float32 [768], replicated
- grad_shift_two: float32 [768], replicated
Inputs may be any that keep to these rules, and one draw needn't show every extreme that they name: `image_counts`: entry f counts the live images among the 4 slots of index f of fsdp; live images come first; entry 0 equals 4.
All inputs are finite; a program needn't handle non-finite values.
Results may differ from a plain program's by a relative error of at most 0.015.
Values may be sent and summed in bfloat16 or wider, within the bound.
A program may use at most 128 MiB of HBM per device.

v0:
```python
import jax
import jax.numpy as jnp
from jax import lax
from jax.sharding import PartitionSpec as P

HEAD_DIM = 64
SEQ = 197
EPS = 1e-06
INV_ROOT_TWO = 0.7071067811865476
INV_ROOT_TWO_PI = 0.3989422804014327


def layer_norm(values, gain, shift):
    center = values - jnp.mean(values, axis=-1, keepdims=True)
    scale_inv = lax.rsqrt(jnp.mean(center * center, axis=-1, keepdims=True) + EPS)
    normal = center * scale_inv
    return (normal, scale_inv, normal * gain + shift)


def norm_back(incoming, normal, scale_inv, gain):
    scaled = incoming * gain
    return scale_inv * (
        scaled
        - jnp.mean(scaled, axis=-1, keepdims=True)
        - normal * jnp.mean(scaled * normal, axis=-1, keepdims=True)
    )


def gelu_parts(pre):
    cdf = 0.5 * (1.0 + lax.erf(pre * INV_ROOT_TWO))
    dens = jnp.exp(-0.5 * pre * pre) * INV_ROOT_TWO_PI
    return (pre * cdf, cdf + pre * dens)


def dotf(left, right):
    return jnp.dot(left, right, preferred_element_type=jnp.float32)


def score_of(query, key):
    return jnp.einsum(
        "bqhe,bkhe->bhqk", query, key, preferred_element_type=jnp.float32
    ) * HEAD_DIM ** (-0.5)


def attend(query, key, value):
    scores = score_of(query, key)
    peak = jnp.max(scores, axis=-1, keepdims=True)
    lse = peak + jnp.log(jnp.sum(jnp.exp(scores - peak), axis=-1, keepdims=True))
    probs = jnp.exp(scores - lse).astype(jnp.bfloat16)
    attended = jnp.einsum("bhqk,bkhe->bqhe", probs, value, preferred_element_type=jnp.float32)
    return (attended.astype(jnp.bfloat16), lse)


def attend_back(query, key, value, lse, attended, dattended):
    scale = HEAD_DIM ** (-0.5)
    delta = jnp.sum(dattended.astype(jnp.float32) * attended.astype(jnp.float32), axis=-1)
    delta = jnp.transpose(delta, (0, 2, 1))[..., None]
    probs_f = jnp.exp(score_of(query, key) - lse)
    probs = probs_f.astype(jnp.bfloat16)
    dvalue = jnp.einsum("bhqk,bqhe->bkhe", probs, dattended, preferred_element_type=jnp.float32)
    dprobs = jnp.einsum("bqhe,bkhe->bhqk", dattended, value, preferred_element_type=jnp.float32)
    dscores = (probs_f * (dprobs - delta)).astype(jnp.bfloat16)
    dquery = jnp.einsum("bhqk,bkhe->bqhe", dscores, key, preferred_element_type=jnp.float32) * scale
    dkey = jnp.einsum("bhqk,bqhe->bkhe", dscores, query, preferred_element_type=jnp.float32) * scale
    return (dquery, dkey, dvalue)


def spread_slice(vector, full_width, offset):
    return lax.dynamic_update_slice_in_dim(jnp.zeros((full_width,), jnp.float32), vector, offset, 0)


def local(
    tokens,
    cotangent,
    image_counts,
    w_qkv,
    b_query,
    b_value,
    w_out,
    b_out,
    w_up,
    b_up,
    w_down,
    b_down,
    gain_one,
    shift_one,
    gain_two,
    shift_two,
):
    rows = tokens.shape[0]
    width = tokens.shape[1]
    slot = lax.axis_index("tp")
    line = (slot * rows + jnp.arange(rows, dtype=jnp.int32)) // SEQ
    live = (line < image_counts[0]).astype(jnp.float32)[:, None]
    xf = tokens.astype(jnp.float32)
    xh1, rs1, n1 = layer_norm(xf, gain_one, shift_one)
    h1g = lax.all_gather(n1.astype(jnp.bfloat16), "tp", axis=0, tiled=True)
    wq_all, wo_all, wu_all, wd_all = (
        lax.all_gather(w_qkv, "fsdp", axis=1, tiled=True),
        lax.all_gather(w_out, "fsdp", axis=1, tiled=True),
        lax.all_gather(w_up, "fsdp", axis=0, tiled=True),
        lax.all_gather(w_down, "fsdp", axis=1, tiled=True),
    )
    group_rows = h1g.shape[0]
    images = group_rows // SEQ
    head_width = wq_all.shape[2]
    hidden_width = wu_all.shape[1]
    shape4 = (images, SEQ, head_width // HEAD_DIM, HEAD_DIM)
    query = (dotf(h1g, wq_all[0]) + b_query).astype(jnp.bfloat16)
    key = dotf(h1g, wq_all[1]).astype(jnp.bfloat16)
    value = (dotf(h1g, wq_all[2]) + b_value).astype(jnp.bfloat16)
    q4, k4, v4 = (query.reshape(shape4), key.reshape(shape4), value.reshape(shape4))
    att4, lse = attend(q4, k4, v4)
    attended = att4.reshape(group_rows, head_width)
    mid = (
        xf
        + lax.psum_scatter(
            dotf(attended, wo_all).astype(jnp.bfloat16), "tp", scatter_dimension=0, tiled=True
        ).astype(jnp.float32)
        + b_out
    )
    xh2, rs2, n2 = layer_norm(mid, gain_two, shift_two)
    h2g = lax.all_gather(n2.astype(jnp.bfloat16), "tp", axis=0, tiled=True)
    pre = dotf(h2g, wu_all) + b_up
    gel, slope = gelu_parts(pre)
    act = gel.astype(jnp.bfloat16)
    block_out = (
        (
            mid
            + lax.psum_scatter(
                dotf(act, wd_all).astype(jnp.bfloat16), "tp", scatter_dimension=0, tiled=True
            ).astype(jnp.float32)
            + b_down
        )
        * live
    ).astype(jnp.bfloat16)
    dout = (cotangent.astype(jnp.float32) * live).astype(jnp.bfloat16)
    doutf = dout.astype(jnp.float32)
    dout_g = lax.all_gather(dout, "tp", axis=0, tiled=True)
    g_down = dotf(act.T, dout_g)
    dpre = dotf(dout_g, wd_all.T) * slope
    g_bup = jnp.sum(dpre, axis=0)
    dpre_b = dpre.astype(jnp.bfloat16)
    g_up = dotf(h2g.T, dpre_b)
    dn2 = lax.psum_scatter(
        dotf(dpre_b, wu_all.T).astype(jnp.bfloat16), "tp", scatter_dimension=0, tiled=True
    ).astype(jnp.float32)
    dmid = doutf + norm_back(dn2, xh2, rs2, gain_two)
    dmid_g = lax.all_gather(dmid.astype(jnp.bfloat16), "tp", axis=0, tiled=True)
    g_out = dotf(attended.T, dmid_g)
    datt = dotf(dmid_g, wo_all.T).astype(jnp.bfloat16)
    dq4, dk4, dv4 = attend_back(q4, k4, v4, lse, att4, datt.reshape(shape4))
    dquery = dq4.reshape(group_rows, head_width)
    dkey = dk4.reshape(group_rows, head_width)
    dvalue = dv4.reshape(group_rows, head_width)
    g_bq = jnp.sum(dquery, axis=0)
    g_bv = jnp.sum(dvalue, axis=0)
    dq_b, dk_b, dv_b = (
        dquery.astype(jnp.bfloat16),
        dkey.astype(jnp.bfloat16),
        dvalue.astype(jnp.bfloat16),
    )
    g_qkv = jnp.stack([dotf(h1g.T, dq_b), dotf(h1g.T, dk_b), dotf(h1g.T, dv_b)])
    dn1_part = dotf(dq_b, wq_all[0].T) + dotf(dk_b, wq_all[1].T) + dotf(dv_b, wq_all[2].T)
    dn1 = lax.psum_scatter(
        dn1_part.astype(jnp.bfloat16), "tp", scatter_dimension=0, tiled=True
    ).astype(jnp.float32)
    grad_tokens = dmid + norm_back(dn1, xh1, rs1, gain_one)
    s_qkv, s_out, s_up, s_down = (
        lax.psum_scatter(g_qkv, "fsdp", scatter_dimension=1, tiled=True),
        lax.psum_scatter(g_out, "fsdp", scatter_dimension=1, tiled=True),
        lax.psum_scatter(g_up, "fsdp", scatter_dimension=0, tiled=True),
        lax.psum_scatter(g_down, "fsdp", scatter_dimension=1, tiled=True),
    )
    head_start = slot * head_width
    hidden_start = slot * hidden_width
    sums = lax.psum(
        (
            spread_slice(g_bq, width, head_start),
            spread_slice(g_bv, width, head_start),
            jnp.sum(dmid, axis=0),
            spread_slice(g_bup, hidden_width * lax.axis_size("tp"), hidden_start),
            jnp.sum(doutf, axis=0),
            jnp.sum(dn1 * xh1, axis=0),
            jnp.sum(dn1, axis=0),
            jnp.sum(dn2 * xh2, axis=0),
            jnp.sum(dn2, axis=0),
        ),
        ("fsdp", "tp"),
    )
    (
        full_bq,
        full_bv,
        sum_bout,
        full_bup,
        sum_bdown,
        sum_gain1,
        sum_shift1,
        sum_gain2,
        sum_shift2,
    ) = sums
    part_bq = lax.dynamic_slice_in_dim(full_bq, head_start, head_width, 0)
    part_bv = lax.dynamic_slice_in_dim(full_bv, head_start, head_width, 0)
    part_bup = lax.dynamic_slice_in_dim(full_bup, hidden_start, hidden_width, 0)
    return (
        block_out,
        grad_tokens,
        s_qkv,
        s_out,
        s_up,
        s_down,
        part_bq,
        part_bv,
        sum_bout,
        part_bup,
        sum_bdown,
        sum_gain1,
        sum_shift1,
        sum_gain2,
        sum_shift2,
    )


def solution(mesh):
    return jax.shard_map(
        local,
        mesh=mesh,
        in_specs=(
            P(("fsdp", "tp"), None),
            P(("fsdp", "tp"), None),
            P("fsdp"),
            P(None, "fsdp", "tp"),
            P("tp"),
            P("tp"),
            P("tp", "fsdp"),
            P(),
            P("fsdp", "tp"),
            P("tp"),
            P("tp", "fsdp"),
            P(),
            P(),
            P(),
            P(),
            P(),
        ),
        out_specs=(
            P(("fsdp", "tp"), None),
            P(("fsdp", "tp"), None),
            P(None, "fsdp", "tp"),
            P("tp", "fsdp"),
            P("fsdp", "tp"),
            P("tp", "fsdp"),
            P("tp"),
            P("tp"),
            P(),
            P("tp"),
            P(),
            P(),
            P(),
            P(),
            P(),
        ),
        check_vma=False,
    )
```

profile of v0, /device:TPU:0, one launch (start us, length us, event | category | flops | bytes accessed | tf_op | source)
XLA Modules:
  0.0 862.7 jit_solution(6002927517635013489)
XLA Ops:
  14.4 45.9 %all_gather.26 = bf16[384,768]{0,1:T(8,128)(2,1)S(1)} all-gather(bf16[384,48]{0,1:T(8,128)(2,1)S(1)} %copy-done.34), channel_id=1, replica_groups=mesh['fsdp'=16,'tp'=2] {'fsdp'}, dimensions={1}, use_global_device_ids=true | all-gather | bytes 626688 | tf_op jit(solution)/shard_map/all_gather | solution.py:100
  62.1 24.3 %all-gather.12.cloned.1.call-done = bf16[3,768,384]{2,1,0:T(8,128)(2,1)} async-done(((bf16[3,48,384]{2,1,0:T(8,128)(2,1)}), bf16[3,768,384]{2,1,0:T(8,128)(2,1)}) %all-gather.12.cloned.1.call-update) | async-done | bytes 1769488 | tf_op jit(solution)/shard_map/all_gather | solution.py:99
  92.2 3.0 convolution_convert_fusion.5
  95.2 3.0 reshape.148
  109.2 3.8 fusion.22
  115.9 4.2 fusion
  123.9 3.1 concatenate
  130.5 2.6 reshape.139
  133.1 4.4 all-gather.20.cloned.1.call-done
  139.0 64.6 %all-gather.14.cloned.1.call-done = bf16[768,1536]{1,0:T(8,128)(2,1)} async-done(((bf16[48,1536]{1,0:T(8,128)(2,1)}), bf16[768,1536]{1,0:T(8,128)(2,1)}) %all-gather.14.cloned.1.call-update) | async-done | bytes 2359312 | tf_op jit(solution)/shard_map/all_gather | solution.py:101
  203.6 6.3 multiply_convert_fusion.1
  209.9 57.5 %all-gather.16.cloned.1.call-done = bf16[1536,768]{0,1:T(8,128)(2,1)} async-done(((bf16[1536,48]{0,1:T(8,128)(2,1)}), bf16[1536,768]{0,1:T(8,128)(2,1)}) %all-gather.16.cloned.1.call-update) | async-done | bytes 2359312 | tf_op jit(solution)/shard_map/all_gather | solution.py:102
  267.4 5.9 fusion.56
  276.8 4.0 fusion.2
  288.4 8.2 all-gather.24.cloned.1.call-done
  299.2 3.0 convolution_convert_fusion.4
  308.7 4.6 bitcast_convert_fusion
  314.7 2.7 convert_element_type.150
  319.0 3.8 multiply_convert_fusion
  325.9 2.7 convert_element_type.148
  328.6 3.5 bitcast_convert_fusion.1
  341.2 6.9 fusion.37
  348.2 6.9 fusion.58
  355.4 5.7 convolution_convert_fusion.1
  365.2 6.8 fusion.54
  378.7 3.1 concatenate.3
  382.7 42.6 %all-reduce.8 = (f32[768]{0:T(1024)S(1)}, f32[768]{0:T(1024)S(1)}, f32[768]{0:T(1024)}, f32[3072]{0:T(1024)S(1)}, f32[768]{0:T(1024)}, /*index=5*/f32[768]{0:T(1...) all-reduce(f32[768]{0:T(1024)S(1)} %dynamic_update_slice.9, ...), channel_id=1, replica_groups=mesh['fsdp'=16,'tp'=2] {'fsdp','tp'}, use_global_device_ids=true, to_apply=%region_20.21 | all-reduce | flops 9216 | bytes 73728 | tf_op jit(solution)/shard_map/psum | solution.py:177
  427.2 4.9 concatenate.1
  432.1 3.5 fusion.28
  435.6 135.8 %reduce-scatter.13.cloned.1.call-done = f32[3,48,384]{2,1,0:T(8,128)} async-done(((f32[3,768,384]{2,1,0:T(8,128)}), f32[3,48,384]{2,1,0:T(8,128)}) %reduce-scatter.13.cloned.1.call-update) | async-done | bytes 221200 | tf_op jit(solution)/shard_map/reduce_scatter | solution.py:170
  571.4 141.7 %reduce-scatter.17.cloned.1.call-done = f32[48,1536]{1,0:T(8,128)} async-done(((f32[768,1536]{1,0:T(8,128)}), f32[48,1536]{1,0:T(8,128)}) %reduce-scatter.17.cloned.1.call-update) | async-done | bytes 294928 | tf_op jit(solution)/shard_map/reduce_scatter | solution.py:172
  713.1 142.6 %reduce-scatter.19.cloned.1.call-done = f32[1536,48]{0,1:T(8,128)} async-done(((f32[1536,768]{0,1:T(8,128)}), f32[1536,48]{0,1:T(8,128)}) %reduce-scatter.19.cloned.1.call-update) | async-done | bytes 294928 | tf_op jit(solution)/shard_map/reduce_scatter | solution.py:173
  (192 shorter events, 84.9 us)
Async XLA Ops:
  7.2 53.1 %all-gather.18.cloned.1.call-start = ((), (), s32[]{:S(2)}) async-start(), calls=%async_computation.11 | async-start | bytes 1843200 | tf_op jit(solution)/shard_map/all_gather | solution.py:97
  8.6 4.1 copy-start.20
  11.2 75.2 %all-gather.12.cloned.1.call-start = ((), (), s32[]{:S(2)}) async-start(), calls=%async_computation.4 | async-start | bytes 1880064 | tf_op jit(solution)/shard_map/all_gather | solution.py:99
  12.0 118.5 %all-gather.22.cloned.1.call-start = ((), (), s32[]{:S(2)}) async-start(), calls=%async_computation.13 | async-start | bytes 1843200 | tf_op jit(solution)/shard_map/all_gather | solution.py:139
  14.3 123.1 %all-gather.20.cloned.1.call-start = ((), (), s32[]{:S(2)}) async-start(), calls=%async_computation.12 | async-start | bytes 1843200 | tf_op jit(solution)/shard_map/all_gather | solution.py:123
  60.3 54.7 %copy-start.23 = (bf16[384,768]{0,1:T(8,128)(2,1)}, bf16[384,768]{0,1:T(8,128)(2,1)S(1)}, u32[]{:S(2)}) copy-start(bf16[384,768]{0,1:T(8,128)(2,1)S(1)} %all_gather.26) | copy-start | bytes 1769476
  60.3 26.1 %copy-start.42 = (f32[384]{0:T(512)S(1)}, f32[384]{0:T(512)}, u32[]{:S(2)}) copy-start(f32[384]{0:T(512)} %param.20) | copy-start | bytes 4612
  62.1 30.1 %copy-start.26 = (bf16[788,768]{1,0:T(8,128)(2,1)}, bf16[788,768]{1,0:T(8,128)(2,1)S(1)}, u32[]{:S(2)}) copy-start(bf16[788,768]{1,0:T(8,128)(2,1)S(1)} %reshape.135) | copy-start | bytes 3631108
  92.2 7.9 copy-start.8
  115.9 6.7 copy-start.39
  115.9 11.0 %copy-start.31 = (f32[768]{0:T(1024)S(1)}, f32[768]{0:T(1024)}, u32[]{:S(2)}) copy-start(f32[768]{0:T(1024)} %param.23) | copy-start | bytes 9220
  120.1 3.7 collective-permute-start
  129.2 74.3 %all-gather.14.cloned.1.call-start = ((), (), s32[]{:S(2)}) async-start(), calls=%async_computation.5 | async-start | bytes 2506752 | tf_op jit(solution)/shard_map/all_gather | solution.py:101
  129.8 137.5 %all-gather.16.cloned.1.call-start = ((), (), s32[]{:S(2)}) async-start(), calls=%async_computation.6 | async-start | bytes 2506752 | tf_op jit(solution)/shard_map/all_gather | solution.py:102
  130.4 166.3 %all-gather.24.cloned.1.call-start = ((), (), s32[]{:S(2)}) async-start(), calls=%async_computation.14 | async-start | bytes 1843200 | tf_op jit(solution)/shard_map/all_gather | solution.py:149
  133.1 70.5 %copy-start.41 = (f32[1536]{0:T(1024)S(1)}, f32[1536]{0:T(1024)}, u32[]{:S(2)}) copy-start(f32[1536]{0:T(1024)} %param.25) | copy-start | bytes 18436
  139.0 70.9 %copy-start.11 = (bf16[788,768]{1,0:T(8,128)(2,1)}, bf16[788,768]{1,0:T(8,128)(2,1)S(1)}, u32[]{:S(2)}) copy-start(bf16[788,768]{1,0:T(8,128)(2,1)S(1)} %reshape.137) | copy-start | bytes 3631108
  267.4 7.3 copy-start.40
  280.8 3.1 collective-permute-start.2
  288.4 10.9 %copy-start.24 = (bf16[384,768]{0,1:T(8,128)(2,1)S(1)}, bf16[384,768]{0,1:T(8,128)(2,1)}, u32[]{:S(2)}) copy-start(bf16[384,768]{0,1:T(8,128)(2,1)} %copy-done.23) | copy-start | bytes 1769476
  288.4 147.2 %reduce-scatter.15.cloned.1.call-start = ((), (), s32[]{:S(2)}) async-start(), calls=%async_computation.8 | async-start | bytes 1253376 | tf_op jit(solution)/shard_map/reduce_scatter | solution.py:171
  308.4 263.0 %reduce-scatter.13.cloned.1.call-start = ((), (), s32[]{:S(2)}) async-start(), calls=%async_computation.7 | async-start | bytes 3760128 | tf_op jit(solution)/shard_map/reduce_scatter | solution.py:170
  324.3 4.2 copy-start.7
  340.9 372.2 %reduce-scatter.17.cloned.1.call-start = ((), (), s32[]{:S(2)}) async-start(), calls=%async_computation.9 | async-start | bytes 5013504 | tf_op jit(solution)/shard_map/reduce_scatter | solution.py:172
  348.1 507.6 %reduce-scatter.19.cloned.1.call-start = ((), (), s32[]{:S(2)}) async-start(), calls=%async_computation.10 | async-start | bytes 5013504 | tf_op jit(solution)/shard_map/reduce_scatter | solution.py:173
  355.4 5.7 copy-start.25
  372.1 4.9 copy-start.18
  372.1 4.5 copy-start.10
  372.9 5.8 collective-permute-start.3
  376.9 50.3 %collective-permute-start.1 = (bf16[6,768]{1,0:T(8,128)(2,1)S(1)}, bf16[6,768]{1,0:T(8,128)(2,1)S(1)}, u32[]{:S(2)}, u32[]{:S(2)}) collective-permute-start(bf16[6,768]{1,0:T(8,128)(2,1)S(1)} %slice.19), channel_id=1, source_target_pairs={{0,1},{2,3},{4,5},{6,7},{8,9},{10,11},{12,13},{14,15},{16,17},{18,... | collective-permute-start | bytes 27656
  378.7 4.0 copy-start.35
  381.8 50.4 %copy-start.38 = (f32[768]{0:T(1024)S(1)}, f32[768]{0:T(1024)}, u32[]{:S(2)}) copy-start(f32[768]{0:T(1024)} %param.27) | copy-start | bytes 9220
  (27 other events, 56.6 us)
Sparse Core Ops, SparseCore 0:
  11.3 11.9 all-gather.17
  26.0 60.3 all-gather.11
  87.9 8.0 all-gather.21
  129.4 8.0 all-gather.19
  140.1 63.4 all-gather.13
  206.2 61.0 all-gather.15
  288.5 8.1 all-gather.23
  308.6 124.7 reduce-scatter.14
  439.1 132.3 reduce-scatter.12
  577.0 136.0 reduce-scatter.16
  719.7 135.9 reduce-scatter.18
where the time goes:
time: 873 us; the launch traced here: 863 us
  waiting for transfers between devices  582 us (67%)
  blocking collectives  104 us (12%)
  matrix products  72 us (8%)
  local copies, waits for them, and re-layouts  58.7 us (7%)
  other arithmetic  21.3 us (2%)
  between operations  16.4 us (2%)
  starting transfers between devices  9.01 us (1%)
    reduce_scatter x1, waiting for transfers between devices, local(): lax.psum_scatter(g_down, 'fsdp', scatter_dimension=1, tiled=True)  143 us
    reduce_scatter x1, waiting for transfers between devices, local(): lax.psum_scatter(g_up, 'fsdp', scatter_dimension=0, tiled=True)  142 us
    reduce_scatter x1, waiting for transfers between devices, local(): lax.psum_scatter(g_qkv, 'fsdp', scatter_dimension=1, tiled=True)  136 us
    all_gather x1, waiting for transfers between devices, local(): lax.all_gather(w_up, 'fsdp', axis=0, tiled=True)  64.6 us
    all_gather x1, waiting for transfers between devices, local(): lax.all_gather(w_down, 'fsdp', axis=1, tiled=True)  57.5 us
    dot_general x18, matrix products, dotf(): return jnp.dot(left, right, preferred_element_type=jnp.float32)  54.5 us
    all_gather x1, blocking collectives, local(): lax.all_gather(w_out, 'fsdp', axis=1, tiled=True)  45.9 us
    psum x1, blocking collectives, local(): lax.psum((spread_slice(g_bq, width, head_start), spread_slice(g_bv, width...  42.6 us
  transfers between devices with their start and end apart: 15, of which 9 were waited for; matrix products, arithmetic and copies ran while one was open for 15% of the time, Pallas kernels for 0%

commit v1 on v0

--- a/solution.py
+++ b/solution.py
@@ -2,6 +2,7 @@
 import jax.numpy as jnp
 from jax import lax
 from jax.sharding import PartitionSpec as P
+from jax.lax import psum
 
 HEAD_DIM = 64
 SEQ = 197
@@ -174,20 +175,19 @@
     )
     head_start = slot * head_width
     hidden_start = slot * hidden_width
-    sums = lax.psum(
-        (
-            spread_slice(g_bq, width, head_start),
-            spread_slice(g_bv, width, head_start),
-            jnp.sum(dmid, axis=0),
-            spread_slice(g_bup, hidden_width * lax.axis_size("tp"), hidden_start),
-            jnp.sum(doutf, axis=0),
-            jnp.sum(dn1 * xh1, axis=0),
-            jnp.sum(dn1, axis=0),
-            jnp.sum(dn2 * xh2, axis=0),
-            jnp.sum(dn2, axis=0),
-        ),
-        ("fsdp", "tp"),
-    )
+    sums = (
+        spread_slice(g_bq, width, head_start),
+        spread_slice(g_bv, width, head_start),
+        jnp.sum(dmid, axis=0),
+        spread_slice(g_bup, hidden_width * lax.axis_size("tp"), hidden_start),
+        jnp.sum(doutf, axis=0),
+        jnp.sum(dn1 * xh1, axis=0),
+        jnp.sum(dn1, axis=0),
+        jnp.sum(dn2 * xh2, axis=0),
+        jnp.sum(dn2, axis=0),
+    )
+    for j in ("tp", "fsdp"):
+        sums = psum(sums, j)
     (
         full_bq,
         full_bv,

time: 873 us -> 868 us (level)
  blocking collectives: 104 us -> 147 us
  waiting for transfers between devices: 582 us -> 540 us
    psum x1 -> x2, blocking collectives: 42.6 us -> 81.9 us  [local(): sums = psum(sums, j)]
    reduce_scatter x1, waiting for transfers between devices: 136 us -> 96.6 us  [local(): lax.psum_scatter(g_qkv, 'fsdp', scatter_dimension=1, tiled=True)]
    unnamed x101 -> x97, local copies, waits for them, and re-layouts: 27.2 us -> 25.4 us
  transfers between devices with their start and end apart: 15 -> 15, of which waited for: 9 -> 9; matrix products, arithmetic and copies ran while one was open for 15% -> 14% of each run, Pallas kernels for 0% -> 0%
where the time goes in v1:
time: 868 us; the launch traced here: 858 us
  waiting for transfers between devices  540 us (62%)
  blocking collectives  147 us (17%)
  matrix products  72.4 us (8%)
  local copies, waits for them, and re-layouts  52.9 us (6%)
  other arithmetic  20.7 us (2%)
  between operations  16.3 us (2%)
  starting transfers between devices  8.83 us (1%)
    reduce_scatter x1, waiting for transfers between devices, local(): lax.psum_scatter(g_down, 'fsdp', scatter_dimension=1, tiled=True)  143 us
    reduce_scatter x1, waiting for transfers between devices, local(): lax.psum_scatter(g_up, 'fsdp', scatter_dimension=0, tiled=True)  142 us
    reduce_scatter x1, waiting for transfers between devices, local(): lax.psum_scatter(g_qkv, 'fsdp', scatter_dimension=1, tiled=True)  96.6 us
    psum x2, blocking collectives, local(): sums = psum(sums, j)  81.9 us
    all_gather x1, waiting for transfers between devices, local(): lax.all_gather(w_up, 'fsdp', axis=0, tiled=True)  64.6 us
    all_gather x1, waiting for transfers between devices, local(): lax.all_gather(w_down, 'fsdp', axis=1, tiled=True)  57.5 us
    dot_general x18, matrix products, dotf(): return jnp.dot(left, right, preferred_element_type=jnp.float32)  55 us
    all_gather x1, blocking collectives, local(): lax.all_gather(w_out, 'fsdp', axis=1, tiled=True)  49.5 us
  transfers between devices with their start and end apart: 15, of which 9 were waited for; matrix products, arithmetic and copies ran while one was open for 14% of the time, Pallas kernels for 0%

profile of v1, /device:TPU:0, one launch (start us, length us, event | category | flops | bytes accessed | tf_op | source)
XLA Modules:
  0.0 858.0 jit_solution(12154536813779960841)
XLA Ops:
  13.8 49.5 %all_gather.26 = bf16[384,768]{0,1:T(8,128)(2,1)} all-gather(bf16[384,48]{0,1:T(8,128)(2,1)S(1)} %copy-done.33), channel_id=1, replica_groups=mesh['fsdp'=16,'tp'=2] {'fsdp'}, dimensions={1}, use_global_device_ids=true | all-gather | bytes 626688 | tf_op jit(solution)/shard_map/all_gather | solution.py:101
  64.9 21.6 %all-gather.12.cloned.1.call-done = bf16[3,768,384]{2,1,0:T(8,128)(2,1)} async-done(((bf16[3,48,384]{2,1,0:T(8,128)(2,1)}), bf16[3,768,384]{2,1,0:T(8,128)(2,1)}) %all-gather.12.cloned.1.call-update) | async-done | bytes 1769488 | tf_op jit(solution)/shard_map/all_gather | solution.py:100
  86.4 2.7 fusion.21
  92.3 2.6 convolution_convert_fusion.5
  105.7 3.8 fusion.22
  112.5 4.3 fusion
  125.3 2.6 reshape.139
  127.9 4.3 all-gather.20.cloned.1.call-done
  133.8 64.6 %all-gather.14.cloned.1.call-done = bf16[768,1536]{1,0:T(8,128)(2,1)} async-done(((bf16[48,1536]{1,0:T(8,128)(2,1)}), bf16[768,1536]{1,0:T(8,128)(2,1)}) %all-gather.14.cloned.1.call-update) | async-done | bytes 2359312 | tf_op jit(solution)/shard_map/all_gather | solution.py:102
  198.4 6.3 multiply_convert_fusion.1
  204.6 57.5 %all-gather.16.cloned.1.call-done = bf16[1536,768]{0,1:T(8,128)(2,1)} async-done(((bf16[1536,48]{0,1:T(8,128)(2,1)}), bf16[1536,768]{0,1:T(8,128)(2,1)}) %all-gather.16.cloned.1.call-update) | async-done | bytes 2359312 | tf_op jit(solution)/shard_map/all_gather | solution.py:103
  262.2 5.9 fusion.56
  271.6 4.0 fusion.2
  283.2 8.2 all-gather.24.cloned.1.call-done
  294.0 3.0 convolution_convert_fusion.4
  303.5 4.6 bitcast_convert_fusion
  309.6 2.7 convert_element_type.150
  313.9 3.8 multiply_convert_fusion
  320.7 2.7 convert_element_type.148
  323.4 3.5 bitcast_convert_fusion.1
  336.0 6.9 fusion.37
  343.0 6.9 fusion.58
  350.2 5.7 convolution_convert_fusion.1
  360.0 6.8 fusion.54
  373.5 3.1 concatenate.3
  377.4 3.5 all-reduce.9
  381.0 78.3 %all-reduce.8 = (f32[768]{0:T(1024)S(1)}, f32[768]{0:T(1024)S(1)}, f32[768]{0:T(1024)}, f32[3072]{0:T(1024)S(1)}, f32[768]{0:T(1024)}, /*index=5*/f32[768]{0:T(1...) all-reduce(f32[768]{0:T(1024)S(1)} %get-tuple-element.32, ...), channel_id=1, replica_groups=mesh['fsdp'=16,'tp'=2] {'fsdp'}, use_global_device_ids=true, to_apply=%region_21.22 | all-reduce | flops 9216 | bytes 73728 | tf_op jit(solution)/shard_map/psum | solution.py:190
  461.3 5.0 concatenate.1
  466.3 3.4 fusion.28
  469.7 96.6 %reduce-scatter.13.cloned.1.call-done = f32[3,48,384]{2,1,0:T(8,128)} async-done(((f32[3,768,384]{2,1,0:T(8,128)}), f32[3,48,384]{2,1,0:T(8,128)}) %reduce-scatter.13.cloned.1.call-update) | async-done | bytes 221200 | tf_op jit(solution)/shard_map/reduce_scatter | solution.py:171
  566.3 141.9 %reduce-scatter.17.cloned.1.call-done = f32[48,1536]{1,0:T(8,128)} async-done(((f32[768,1536]{1,0:T(8,128)}), f32[48,1536]{1,0:T(8,128)}) %reduce-scatter.17.cloned.1.call-update) | async-done | bytes 294928 | tf_op jit(solution)/shard_map/reduce_scatter | solution.py:173
  708.3 142.8 %reduce-scatter.19.cloned.1.call-done = f32[1536,48]{0,1:T(8,128)} async-done(((f32[1536,768]{0,1:T(8,128)}), f32[1536,48]{0,1:T(8,128)}) %reduce-scatter.19.cloned.1.call-update) | async-done | bytes 294928 | tf_op jit(solution)/shard_map/reduce_scatter | solution.py:174
  (189 shorter events, 82.6 us)
Async XLA Ops:
  7.2 56.1 %all-gather.18.cloned.1.call-start = ((), (), s32[]{:S(2)}) async-start(), calls=%async_computation.11 | async-start | bytes 1843200 | tf_op jit(solution)/shard_map/all_gather | solution.py:98
  8.6 4.1 copy-start.19
  11.2 75.2 %all-gather.12.cloned.1.call-start = ((), (), s32[]{:S(2)}) async-start(), calls=%async_computation.4 | async-start | bytes 1880064 | tf_op jit(solution)/shard_map/all_gather | solution.py:100
  12.0 113.4 %all-gather.22.cloned.1.call-start = ((), (), s32[]{:S(2)}) async-start(), calls=%async_computation.13 | async-start | bytes 1843200 | tf_op jit(solution)/shard_map/all_gather | solution.py:140
  13.8 118.5 %all-gather.20.cloned.1.call-start = ((), (), s32[]{:S(2)}) async-start(), calls=%async_computation.12 | async-start | bytes 1843200 | tf_op jit(solution)/shard_map/all_gather | solution.py:124
  63.3 23.1 %copy-start.40 = (f32[384]{0:T(512)S(1)}, f32[384]{0:T(512)}, u32[]{:S(2)}) copy-start(f32[384]{0:T(512)} %param.20) | copy-start | bytes 4612
  64.9 21.6 %copy-start.25 = (bf16[788,768]{1,0:T(8,128)(2,1)}, bf16[788,768]{1,0:T(8,128)(2,1)S(1)}, u32[]{:S(2)}) copy-start(bf16[788,768]{1,0:T(8,128)(2,1)S(1)} %reshape.135) | copy-start | bytes 3631108
  92.3 6.6 copy-start.8
  105.7 3.8 copy-start.3
  112.5 6.6 copy-start.37
  112.5 9.3 %copy-start.30 = (f32[768]{0:T(1024)S(1)}, f32[768]{0:T(1024)}, u32[]{:S(2)}) copy-start(f32[768]{0:T(1024)} %param.23) | copy-start | bytes 9220
  116.8 3.5 collective-permute-start
  124.1 74.3 %all-gather.14.cloned.1.call-start = ((), (), s32[]{:S(2)}) async-start(), calls=%async_computation.5 | async-start | bytes 2506752 | tf_op jit(solution)/shard_map/all_gather | solution.py:102
  124.7 137.5 %all-gather.16.cloned.1.call-start = ((), (), s32[]{:S(2)}) async-start(), calls=%async_computation.6 | async-start | bytes 2506752 | tf_op jit(solution)/shard_map/all_gather | solution.py:103
  125.3 166.2 %all-gather.24.cloned.1.call-start = ((), (), s32[]{:S(2)}) async-start(), calls=%async_computation.14 | async-start | bytes 1843200 | tf_op jit(solution)/shard_map/all_gather | solution.py:150
  127.9 70.4 %copy-start.39 = (f32[1536]{0:T(1024)S(1)}, f32[1536]{0:T(1024)}, u32[]{:S(2)}) copy-start(f32[1536]{0:T(1024)} %param.25) | copy-start | bytes 18436
  133.8 70.9 %copy-start.11 = (bf16[788,768]{1,0:T(8,128)(2,1)}, bf16[788,768]{1,0:T(8,128)(2,1)S(1)}, u32[]{:S(2)}) copy-start(bf16[788,768]{1,0:T(8,128)(2,1)S(1)} %reshape.137) | copy-start | bytes 3631108
  262.2 7.3 copy-start.38
  275.7 3.1 collective-permute-start.2
  283.2 10.9 %copy-start.23 = (bf16[384,768]{0,1:T(8,128)(2,1)S(1)}, bf16[384,768]{0,1:T(8,128)(2,1)}, u32[]{:S(2)}) copy-start(bf16[384,768]{0,1:T(8,128)(2,1)} %all_gather.26) | copy-start | bytes 1769476
  283.2 186.6 %reduce-scatter.15.cloned.1.call-start = ((), (), s32[]{:S(2)}) async-start(), calls=%async_computation.8 | async-start | bytes 1253376 | tf_op jit(solution)/shard_map/reduce_scatter | solution.py:172
  303.3 263.0 %reduce-scatter.13.cloned.1.call-start = ((), (), s32[]{:S(2)}) async-start(), calls=%async_computation.7 | async-start | bytes 3760128 | tf_op jit(solution)/shard_map/reduce_scatter | solution.py:171
  313.9 3.9 copy-start.9
  319.2 4.2 copy-start.7
  335.7 372.5 %reduce-scatter.17.cloned.1.call-start = ((), (), s32[]{:S(2)}) async-start(), calls=%async_computation.9 | async-start | bytes 5013504 | tf_op jit(solution)/shard_map/reduce_scatter | solution.py:173
  342.9 508.1 %reduce-scatter.19.cloned.1.call-start = ((), (), s32[]{:S(2)}) async-start(), calls=%async_computation.10 | async-start | bytes 5013504 | tf_op jit(solution)/shard_map/reduce_scatter | solution.py:174
  350.2 5.7 copy-start.24
  366.9 4.9 copy-start.18
  366.9 4.5 copy-start.10
  367.7 5.8 collective-permute-start.3
  371.7 89.6 %collective-permute-start.1 = (bf16[6,768]{1,0:T(8,128)(2,1)S(1)}, bf16[6,768]{1,0:T(8,128)(2,1)S(1)}, u32[]{:S(2)}, u32[]{:S(2)}) collective-permute-start(bf16[6,768]{1,0:T(8,128)(2,1)S(1)} %slice.19), channel_id=1, source_target_pairs={{0,1},{2,3},{4,5},{6,7},{8,9},{10,11},{12,13},{14,15},{16,17},{18,... | collective-permute-start | bytes 27656
  376.6 89.7 %copy-start.36 = (f32[768]{0:T(1024)S(1)}, f32[768]{0:T(1024)}, u32[]{:S(2)}) copy-start(f32[768]{0:T(1024)} %param.27) | copy-start | bytes 9220
  (25 other events, 45.9 us)
Sparse Core Ops, SparseCore 0:
  11.3 11.9 all-gather.17
  26.0 60.3 all-gather.11
  88.0 8.0 all-gather.21
  124.2 7.9 all-gather.19
  134.9 63.4 all-gather.13
  201.0 61.0 all-gather.15
  283.3 8.1 all-gather.23
  303.4 124.8 reduce-scatter.14
  434.0 132.2 reduce-scatter.12
  571.9 136.3 reduce-scatter.16
  714.8 136.1 reduce-scatter.18
